TPU v7x, 256 devices: a whole 4x4x8 slice. The times are simulated.
256 devices in a mesh: dp: 8 (over x, core), row: 8 (over z), col: 4 (over y).
Axes of the slice: x: 4, y: 4, z: 8, core: 2. Of those that a mesh axis runs over, the one named last changes fastest.
Arguments:
- calib: bfloat16 [4096, 8192], P('dp', 'col'), as said below
- weight: bfloat16 [26624, 8192], P(('dp', 'row'), 'col'), may hold values from -0.0625 to 0.0625
- sketch: bfloat16 [8192, 512], P('col', 'row'), may hold values from -6 to 6
Outputs:
- panels: float32 [26624, 512], P(('dp', 'row'))
- projections: float32 [512, 8192], P(('dp', 'row'), 'col')
Inputs may be any that keep to these rules, and one draw needn't show every extreme that they name: `calib`: each feature and each token has its own scale.
All inputs are finite; a program needn't handle non-finite values.
Results may differ from a plain program's by a relative error of at most 0.0062.
Values may be sent and summed in bfloat16 or wider, within the bound.
No kernel may reach another device: no remote copies, remote signals or barrier semaphores. Data moves between devices by JAX's collectives and lax.ppermute only.
A program may use at most 128 MiB of HBM per device.

v0:
```python
import math

import jax
import jax.numpy as jnp
from jax import lax
from jax.sharding import PartitionSpec as P

WB = 512


damping_ratio = 0.5


def shards(calib, weight, sketch):
    n_data = lax.axis_size("dp")
    n_rows = lax.axis_size("row")
    n_cols = lax.axis_size("col")
    tok_local, tile = calib.shape
    tokens = tok_local * n_data
    width = tile * n_cols
    hidden = weight.shape[0] * n_data * n_rows
    n_blocks = tile // WB
    block = tile // (n_data * n_rows)
    row_index = lax.axis_index("row")
    grouped = calib.reshape(tok_local, n_data, n_rows, block)
    picked = lax.dynamic_index_in_dim(grouped, row_index, 2, keepdims=False)
    starts = (jnp.arange(n_data, dtype=jnp.int32) * n_rows + row_index) * block // WB
    blocks_view = calib.reshape(tok_local, n_blocks, WB)
    selected = jnp.take(blocks_view, starts, axis=1)
    partial_rows = jnp.einsum("tdb,tdw->dbw", picked, selected, preferred_element_type=jnp.float32)
    partial_rows = partial_rows.reshape(n_data * block, WB)
    own_rows = lax.psum_scatter(partial_rows, "dp", scatter_dimension=0, tiled=True)
    first = (lax.axis_index("dp") * n_rows + row_index) * block
    square_part = lax.dynamic_slice_in_dim(own_rows, first % WB, block, 1)
    local_trace = jnp.sum(jnp.diagonal(square_part))
    gram = lax.all_gather(own_rows, ("dp", "row"), axis=0, tiled=True)
    total = lax.psum(local_trace, ("dp", "row", "col"))
    lam = damping_ratio * total / (tokens * width)
    gram = (
        gram.reshape(n_blocks, WB, WB) / tokens + lam * jnp.eye(WB, dtype=jnp.float32)[None, :, :]
    )
    factor = jnp.linalg.cholesky(gram).astype(jnp.bfloat16)
    stacked = sketch.reshape(n_blocks, WB, sketch.shape[1])
    own_mixed = jnp.einsum("kab,kbc->kac", factor, stacked, preferred_element_type=jnp.float32)
    own_mixed = own_mixed.reshape(tile, sketch.shape[1]).astype(jnp.bfloat16)
    mixed = lax.all_gather(own_mixed, "row", axis=1, tiled=True)
    ysum = lax.psum(jnp.dot(weight, mixed, preferred_element_type=jnp.float32), "col")
    local_cross = jnp.dot(ysum.T, ysum, precision=lax.Precision.HIGHEST)
    cross = lax.psum(local_cross, ("dp", "row")) / hidden
    rfac = jnp.linalg.cholesky(cross)
    panels = jax.scipy.linalg.solve_triangular(rfac, ysum.T, lower=True).T
    panel_bf = panels.astype(jnp.bfloat16)
    rank_total = panels.shape[1]
    rows_each = rank_total // (n_data * n_rows)
    moments = lax.psum_scatter(
        lax.dot_general(
            panel_bf, weight, (((0,), (0,)), ((), ())), preferred_element_type=jnp.float32
        ),
        ("dp", "row"),
        scatter_dimension=0,
        tiled=True,
    )
    moments = moments.reshape(rows_each, n_blocks, WB)
    projections = jnp.einsum(
        "rka,kab->rkb", moments, factor.astype(jnp.float32), precision=lax.Precision.HIGHEST
    )
    projections = projections.reshape(rows_each, tile) / math.sqrt(hidden)
    return (panels, projections)


def solution(mesh):
    return jax.shard_map(
        shards,
        mesh=mesh,
        in_specs=(P("dp", "col"), P(("dp", "row"), "col"), P("col", "row")),
        out_specs=(P(("dp", "row"), None), P(("dp", "row"), "col")),
        check_vma=False,
    )
```

profile of v0, /device:TPU:8, one launch (start us, length us, event | category | flops | bytes accessed | tf_op | source)
XLA Modules:
  0.0 1147.4 jit_solution(3493736268372012277)
XLA Ops:
  7.3 4.0 copy.63
  11.3 4.2 copy.65
  15.5 4.3 gather_fusion
  23.8 36.4 %reduce-scatter.2.cloned.1.call-done = f32[32,512]{1,0:T(8,128)} async-done(((f32[256,512]{1,0:T(8,128)}), f32[32,512]{1,0:T(8,128)}) %reduce-scatter.2.cloned.1.call-update) | async-done | bytes 65552 | tf_op jit(solution)/shard_map/reduce_scatter | solution.py:32
  63.8 75.0 %psum.21 = f32[]{:T(128)} all-reduce(f32[]{:T(128)} %reduce_sum.9), channel_id=1, replica_groups=mesh['dp'=8,'row'=8,'col'=4] {'dp','row','col'}, use_global_device_ids=true, to_apply=%region_2.3 | all-reduce | flops 1 | bytes 8 | tf_op jit(solution)/shard_map/psum | solution.py:37
  142.2 4.7 broadcast_multiply_fusion
  146.8 5.2 copy.67
  152.0 4.8 broadcast_add_fusion
  156.8 5.2 copy.68
  162.1 4.6 fusion
  168.7 46.9 %custom-call.62 = f32[4,128,128]{2,1,0:T(8,128)S(1)} custom-call(f32[4,128,128]{2,1,0:T(8,128)S(1)} %cholesky.531), custom_call_target="Cholesky" | custom-call | tf_op jit(solution)/shard_map/jit(cholesky)/cholesky | solution.py:42
  218.1 39.5 %custom-call.63 = f32[4,1,128,128]{2,3,1,0:T(8,128)S(1)} custom-call(f32[4,1,128,128]{3,2,1,0:T(8,128)S(1)} %select_bitcast_fusion.2), custom_call_target="InvertDiagBlocksLowerTriangular" | custom-call | tf_op jit(solution)/shard_map/jit(cholesky)/cholesky | solution.py:42
  262.5 46.9 %custom-call.64 = f32[4,128,128]{2,1,0:T(8,128)S(1)} custom-call(f32[4,128,128]{2,1,0:T(8,128)S(1)} %cholesky.535), custom_call_target="Cholesky" | custom-call | tf_op jit(solution)/shard_map/jit(cholesky)/cholesky | solution.py:42
  310.2 39.3 %custom-call.65 = f32[4,1,128,128]{2,3,1,0:T(8,128)S(1)} custom-call(f32[4,1,128,128]{3,2,1,0:T(8,128)S(1)} %get-tuple-element.27), custom_call_target="InvertDiagBlocksLowerTriangular" | custom-call | tf_op jit(solution)/shard_map/jit(cholesky)/cholesky | solution.py:42
  353.6 47.3 %custom-call.66 = f32[4,128,128]{2,1,0:T(8,128)S(1)} custom-call(f32[4,128,128]{2,1,0:T(8,128)S(1)} %cholesky.540), custom_call_target="Cholesky" | custom-call | tf_op jit(solution)/shard_map/jit(cholesky)/cholesky | solution.py:42
  401.7 39.3 %custom-call.67 = f32[4,1,128,128]{2,3,1,0:T(8,128)S(1)} custom-call(f32[4,1,128,128]{3,2,1,0:T(8,128)S(1)} %get-tuple-element.25), custom_call_target="InvertDiagBlocksLowerTriangular" | custom-call | tf_op jit(solution)/shard_map/jit(cholesky)/cholesky | solution.py:42
  444.7 46.9 %custom-call.68 = f32[4,128,128]{2,1,0:T(8,128)S(1)} custom-call(f32[4,128,128]{2,1,0:T(8,128)S(1)} %convolution_subtract_fusion.2), custom_call_target="Cholesky" | custom-call | tf_op jit(solution)/shard_map/jit(cholesky)/cholesky | solution.py:42
  497.5 38.8 %all-gather.5.cloned.1.call-done = bf16[2048,512]{0,1:T(8,128)(2,1)} async-done(((bf16[2048,64]{0,1:T(8,128)(2,1)}), bf16[2048,512]{0,1:T(8,128)(2,1)}) %all-gather.5.cloned.1.call-update) | async-done | bytes 2097168 | tf_op jit(solution)/shard_map/all_gather | solution.py:46
  540.0 47.8 %all-reduce.7.cloned.1.call-done = f32[416,512]{1,0:T(8,128)} async-done(((f32[416,512]{1,0:T(8,128)}), f32[416,512]{1,0:T(8,128)}) %all-reduce.7.cloned.1.call-update) | async-done | bytes 851984 | tf_op jit(solution)/shard_map/psum | solution.py:47
  587.8 4.3 fusion.59
  592.4 186.7 %all-reduce.9.cloned.1.call-done = f32[512,512]{0,1:T(8,128)} async-done(((f32[512,512]{0,1:T(8,128)}), f32[512,512]{0,1:T(8,128)}) %all-reduce.9.cloned.1.call-update) | async-done | bytes 1048592 | tf_op jit(solution)/shard_map/psum | solution.py:49
  786.6 11.7 %cholesky.467 = f32[128,128]{1,0:T(8,128)S(1)} custom-call(f32[128,128]{1,0:T(8,128)S(1)} %cholesky.544), custom_call_target="Cholesky" | custom-call | tf_op jit(solution)/shard_map/jit(cholesky)/cholesky | solution.py:50
  799.5 9.8 custom-call.69
  812.6 11.7 %cholesky.483 = f32[128,128]{1,0:T(8,128)S(1)} custom-call(f32[128,128]{1,0:T(8,128)S(1)} %cholesky.548), custom_call_target="Cholesky" | custom-call | tf_op jit(solution)/shard_map/jit(cholesky)/cholesky | solution.py:50
  826.2 10.0 custom-call.70
  838.6 11.7 %cholesky.504 = f32[128,128]{1,0:T(8,128)S(1)} custom-call(f32[128,128]{1,0:T(8,128)S(1)} %cholesky.553), custom_call_target="Cholesky" | custom-call | tf_op jit(solution)/shard_map/jit(cholesky)/cholesky | solution.py:50
  851.6 9.8 custom-call.71
  863.6 11.9 %cholesky.521 = f32[128,128]{1,0:T(8,128)S(1)} custom-call(f32[128,128]{1,0:T(8,128)S(1)} %convolution_subtract_fusion.8), custom_call_target="Cholesky" | custom-call | tf_op jit(solution)/shard_map/jit(cholesky)/cholesky | solution.py:50
  881.7 11.6 %while.2 = (s32[]{:T(128)}, f32[512,512]{1,0:T(8,128)}, s32[4,2]{0,1:T(2,128)S(1)}, f32[4,128,128]{2,1,0:T(8,128)S(1)}) while((s32[]{:T(128)}, f32[512,512]{1,0:T(8,128)}, s32[4,2]{0,1:T(2,128)S(1)}, f32[4,128,128]{2,1,0:T(8,128)S(1)}) %tuple.43), condition=%wide.while_cond.clone, body=%wide.while_body.sunk.clone | while | flops 2 | bytes 131173 | solution.py:51
  893.3 39.3 %custom-call.72 = f32[4,128,128]{1,2,0:T(8,128)S(1)} custom-call(f32[4,128,128]{2,1,0:T(8,128)S(1)} %get-tuple-element.9), custom_call_target="InvertDiagBlocksLowerTriangular" | custom-call | tf_op jit(solution)/shard_map/jit(_solve_triangular)/triangular_solve | solution.py:51
  942.9 192.3 %all-reduce.11.cloned.1.call-done = f32[512,2048]{1,0:T(8,128)} async-done(((f32[512,2048]{1,0:T(8,128)}), f32[512,2048]{1,0:T(8,128)}) %all-reduce.11.cloned.1.call-update) | async-done | bytes 4194320
  1136.0 4.1 convolution_multiply_fusion
  (110 shorter events, 84.0 us)
Async XLA Ops:
  7.2 529.2 %copy-start = (bf16[416,2048]{1,0:T(8,128)(2,1)S(1)}, bf16[416,2048]{1,0:T(8,128)(2,1)}, u32[]{:S(2)}) copy-start(bf16[416,2048]{1,0:T(8,128)(2,1)} %param.4) | copy-start | bytes 5111812
  7.2 53.0 %reduce-scatter.2.cloned.1.call-start = ((), (), s32[]{:S(2)}) async-start(), calls=%async_computation.1 | async-start | bytes 589824 | tf_op jit(solution)/shard_map/reduce_scatter | solution.py:32
  23.8 118.4 %all-gather.3.cloned.1.call-start = ((), (), s32[]{:S(2)}) async-start(), calls=%async_computation.2 | async-start | bytes 4259840 | tf_op jit(solution)/shard_map/all_gather | solution.py:36
  60.2 476.1 %all-gather.5.cloned.1.call-start = ((), (), s32[]{:S(2)}) async-start(), calls=%async_computation.3 | async-start | bytes 2359296 | tf_op jit(solution)/shard_map/all_gather | solution.py:46
  166.7 1.9 copy-start.1
  497.5 90.4 %all-reduce.7.cloned.1.call-start = ((), (), s32[]{:S(2)}) async-start(), calls=%async_computation.4 | async-start | bytes 1703936 | tf_op jit(solution)/shard_map/psum | solution.py:47
  539.9 239.2 %all-reduce.9.cloned.1.call-start = ((), (), s32[]{:S(2)}) async-start(), calls=%async_computation.5 | async-start | bytes 2097152 | tf_op jit(solution)/shard_map/psum | solution.py:49
  592.2 543.0 %all-reduce.11.cloned.1.call-start = ((), (), s32[]{:S(2)}) async-start(), calls=%async_computation.6 | async-start | bytes 8388608
  779.1 5.0 copy-start.3
  785.6 1.0 copy-start.5
  786.6 146.1 %copy-start.2 = (f32[416,512]{1,0:T(8,128)S(1)}, f32[416,512]{1,0:T(8,128)}, u32[]{:S(2)}) copy-start(f32[416,512]{1,0:T(8,128)} %all-reduce.7.cloned.1.call-done) | copy-start | bytes 2555908
  938.3 3.3 copy-start.4
  938.3 3.3 copy-start.7
  938.3 197.7 %copy-start.6 = (pred[512,512]{1,0:T(8,128)(4,1)S(1)}, pred[512,512]{1,0:T(8,128)(4,1)}, u32[]{:S(2)}) copy-start(pred[512,512]{1,0:T(8,128)(4,1)} %iota_compare_fusion.1) | copy-start | bytes 786436
Sparse Core Ops, SparseCore 0:
  23.9 36.2 reduce-scatter.1
  63.3 77.7 all-gather.2
  497.6 38.7 all-gather.4
  540.1 47.7 all-reduce.6
  592.3 186.7 all-reduce.8
  941.7 193.4 all-reduce.10
where the time goes:
time: 1160 us; the launch traced here: 1150 us
  waiting for transfers between devices  502 us (43%)
  other arithmetic  454 us (39%)
  blocking collectives  75 us (6%)
  local copies, waits for them, and re-layouts  49 us (4%)
  matrix products  48.4 us (4%)
  between operations  18.7 us (2%)
    another operation x16, other arithmetic, shards(): factor = jnp.linalg.cholesky(gram).astype(jnp.bfloat16)  310 us
    unnamed x7, waiting for transfers between devices  192 us
    psum x1, waiting for transfers between devices, shards(): cross = lax.psum(local_cross, ('dp', 'row')) / hidden  187 us
    another operation x16, other arithmetic, shards(): rfac = jnp.linalg.cholesky(cross)  81.9 us
    psum x1, blocking collectives, shards(): total = lax.psum(local_trace, ('dp', 'row', 'col'))  75 us
    psum x1, waiting for transfers between devices, shards(): lax.psum(jnp.dot(weight, mixed, preferred_element_type=jnp.float32), 'col')  47.8 us
    another operation x4, other arithmetic, shards(): panels = jax.scipy.linalg.solve_triangular(rfac, ysum.T, lower=True).T  42.5 us
    all_gather x1, waiting for transfers between devices, shards(): mixed = lax.all_gather(own_mixed, 'row', axis=1, tiled=True)  38.8 us
  transfers between devices with their start and end apart: 6, of which 5 were waited for; matrix products, arithmetic and copies ran while one was open for 1% of the time, Pallas kernels for 0%

commit v1 on v0

v1 whole, which is shorter than its diff:
```python
import math

import jax
import jax.numpy as jnp
from jax import lax
from jax.experimental import pallas as pl
from jax.experimental.pallas import tpu as pltpu
from jax.sharding import PartitionSpec as P

WB = 512
NB = 128
damping_ratio = 0.5
f32 = jnp.float32
bf16 = jnp.bfloat16
HI = lax.Precision.HIGHEST
PAIRS = [(i, j) for i in range(4) for j in range(i, 4)]
NP = len(PAIRS)
HALF = NP // 2


def tn(a, b, precision=None):
    return lax.dot_general(
        a, b, (((0,), (0,)), ((), ())), preferred_element_type=f32, precision=precision
    )


def nt(a, b, precision=None):
    return lax.dot_general(
        a, b, (((1,), (1,)), ((), ())), preferred_element_type=f32, precision=precision
    )


def nn(a, b, precision=None):
    return jnp.dot(a, b, preferred_element_type=f32, precision=precision)


def call(kernel, out_shape, n_smem, n_vmem, scratch=(), name=None):
    one = not isinstance(out_shape, (tuple, list))
    return pl.pallas_call(
        kernel,
        out_shape=out_shape,
        in_specs=[pl.BlockSpec(memory_space=pltpu.SMEM)] * n_smem
        + [pl.BlockSpec(memory_space=pltpu.VMEM)] * n_vmem,
        out_specs=pl.BlockSpec(memory_space=pltpu.VMEM)
        if one
        else tuple(pl.BlockSpec(memory_space=pltpu.VMEM) for _ in out_shape),
        scratch_shapes=list(scratch),
        compiler_params=pltpu.CompilerParams(vmem_limit_bytes=40 * 2**20),
        name=name,
    )


def shape(s, d=f32):
    return jax.ShapeDtypeStruct(s, d)


def sub(x, j):
    return jnp.broadcast_to(x[j : j + 1, :], (8, NB))


def lane(x, c):
    return jnp.broadcast_to(x[:, c : c + 1], (8, NB))


def diag_factor(rows):
    row = lax.broadcasted_iota(jnp.int32, (8, NB), 0)
    col = lax.broadcasted_iota(jnp.int32, (8, NB), 1)
    upper = list(rows)
    inv = [jnp.where(col == row + 8 * g, 1.0, 0.0).astype(f32) for g in range(16)]
    for g in range(16):
        c = [lane(upper[g], 8 * g + j) for j in range(8)]
        v, z = upper[g], inv[g]
        us, zs, ss, q = [], [], [], {}
        for j in range(8):
            s = lax.rsqrt(sub(c[j], j))
            u = sub(v, j) * s
            w = sub(z, j) * s
            m = jnp.where(row > j, c[j] * s, 0.0)
            for k in range(j + 1, 8):
                q[j, k] = sub(c[k], j) * s
                c[k] = c[k] - m * q[j, k]
            v = jnp.where(row == j, u, v - m * u)
            z = jnp.where(row == j, w, z - m * w)
            us.append(u)
            zs.append(w)
            ss.append(s)
        upper[g] = jnp.where(col >= row + 8 * g, v, 0.0)
        inv[g] = z
        for h in range(g + 1, 16):
            low = []
            for j in range(8):
                t = lane(upper[h], 8 * g + j)
                for k in range(j):
                    t = t - low[k] * q[k, j]
                low.append(t * ss[j])
            a, b = low[0] * us[0], low[0] * zs[0]
            for j in range(1, 8):
                a = a + low[j] * us[j]
                b = b + low[j] * zs[j]
            upper[h] = upper[h] - a
            inv[h] = inv[h] - b
    return upper, inv


def blk(i):
    return slice(NB * i, NB * i + NB)


def factor_blocks(a_ref, u_ref, d_ref, e_ref=None):
    for k in range(4):
        upper, inv = diag_factor([a_ref[NB * k + 8 * g : NB * k + 8 * g + 8, blk(k)] for g in range(16)])
        for g in range(16):
            u_ref[NB * k + 8 * g : NB * k + 8 * g + 8, blk(k)] = upper[g]
            d_ref[8 * g : 8 * g + 8, :] = inv[g]
        dinv = d_ref[...]
        for j in range(k + 1, 4):
            u_ref[blk(k), blk(j)] = nn(dinv, a_ref[blk(k), blk(j)], HI)
        for i in range(k + 1, 4):
            a_ref[blk(i), NB * i :] -= tn(u_ref[blk(k), blk(i)], u_ref[blk(k), NB * i :], HI)
        if e_ref is not None:
            if k:
                e_ref[blk(k), : NB * k] = nn(dinv, e_ref[blk(k), : NB * k], HI)
            e_ref[blk(k), blk(k)] = dinv
            for i in range(k + 1, 4):
                e_ref[blk(i), : NB * (k + 1)] -= tn(u_ref[blk(k), blk(i)], e_ref[blk(k), : NB * (k + 1)], HI)


def gram_kernel(ids, c_ref, o_ref, g_ref):
    r = ids[2]
    row = lax.broadcasted_iota(jnp.int32, (8, NB), 0)
    col = lax.broadcasted_iota(jnp.int32, (8, NB), 1)
    acc = jnp.zeros((8, NB), f32)
    for b in range(4):
        part = c_ref[:, WB * b : WB * b + WB]
        g_ref[...] = tn(part, part)
        for i in range(4):
            for g in range(16):
                tile = g_ref[NB * i + 8 * g : NB * i + 8 * g + 8, blk(i)]
                acc = acc + jnp.where(col == row + 8 * g, tile, 0.0)
        for half in range(2):
            for p, (i, j) in enumerate(PAIRS):
                start = pl.multiple_of(NB * i + 16 * r + 8 * half, 8)
                o_ref[2 * b + half, p] = g_ref[pl.ds(start, 8), blk(j)]
    for d in range(8):
        o_ref[d, NP] = acc


def chol_kernel(scale, lam_scale, ids, own_ref, oth_ref, s0, s1, s2, s3, o_ref, h_ref, a_ref, u_ref, d_ref):
    k = ids[1]
    total = jnp.sum(s0[...] + s1[...] + s2[...] + s3[...], keepdims=True)
    lam = jnp.broadcast_to(total * lam_scale, (8, NB))
    row = lax.broadcasted_iota(jnp.int32, (8, NB), 0)
    col = lax.broadcasted_iota(jnp.int32, (8, NB), 1)
    for half in range(2):
        side = lax.rem(k + half, 2)
        ref = own_ref if half == 0 else oth_ref
        for r in range(8):
            for p, (i, j) in enumerate(PAIRS):
                start = pl.multiple_of(NB * i + 16 * r + 8 * side, 8)
                tile = ref[r, p] * scale
                if i == j:
                    tile = tile + jnp.where(col == row + (16 * r + 8 * side), lam, 0.0)
                a_ref[pl.ds(start, 8), blk(j)] = tile
    factor_blocks(a_ref, u_ref, d_ref)
    for p, (i, j) in enumerate(PAIRS):
        o_ref[p] = u_ref[blk(i), blk(j)].astype(bf16)
    h_ref[...] = o_ref[pl.ds(HALF * k, HALF)]


def mixed_kernel(ids, own_ref, r1, r2, r3, t1, t2, t3, sk_ref, w_ref, y_ref, f_ref, full_ref):
    x, k = ids[0], ids[1]
    full_ref[...] = jnp.zeros((WB, WB), bf16)
    f_ref[0] = own_ref[...]
    for s, (a, b) in enumerate(((r1, t1), (r2, t2), (r3, t3))):
        f_ref[s + 1, pl.ds(HALF * k, HALF)] = a[...]
        f_ref[s + 1, pl.ds(HALF * (1 - k), HALF)] = b[...]
    for s in range(4):
        b = lax.rem(x - s + 4, 4)
        for p, (i, j) in enumerate(PAIRS):
            full_ref[blk(i), blk(j)] = f_ref[s, p]
        cols = pl.ds(pl.multiple_of(WB * b, WB), WB)
        mixed = tn(full_ref[...], sk_ref[cols, :]).astype(bf16)
        y = nn(w_ref[:, cols], mixed)
        if s == 0:
            y_ref[...] = y
        else:
            y_ref[...] += y


def cross_kernel(ids, y_ref, own_ref, oth_ref, ys_ref):
    k = ids[1]
    y = (y_ref[0] + y_ref[1]) + (y_ref[2] + y_ref[3])
    ys_ref[...] = y
    for side in range(2):
        blocks = [nn_t(y[:, blk(i)], y[:, blk(j)]) for i, j in PAIRS[HALF * side : HALF * side + HALF]]

        def put(ref, blocks=blocks):
            for q, c in enumerate(blocks):
                for g in range(16):
                    ref[g, q] = c[8 * g : 8 * g + 8, :]

        pl.when(k == side)(lambda: put(own_ref))
        pl.when(k != side)(lambda: put(oth_ref))


def nn_t(a, b):
    return tn(a, b, HI)


def chol2_kernel(scale, ids, own_ref, oth_ref, o_ref, a_ref, u_ref, d_ref):
    k = ids[1]

    def put(first, second):
        for side, ref in enumerate((first, second)):
            for q, (i, j) in enumerate(PAIRS[HALF * side : HALF * side + HALF]):
                for g in range(16):
                    a_ref[NB * i + 8 * g : NB * i + 8 * g + 8, blk(j)] = ref[g, q] * scale

    pl.when(k == 0)(lambda: put(own_ref, oth_ref))
    pl.when(k != 0)(lambda: put(oth_ref, own_ref))
    o_ref[...] = jnp.zeros((WB, WB), f32)
    factor_blocks(a_ref, u_ref, d_ref, o_ref)


def moment_kernel(ids, y0, y1, y2, y3, w_ref, own_ref, oth_ref, y_ref, yb_ref):
    x, k, c = ids[0], ids[1], ids[3]
    n = y0.shape[0]
    for s, ref in enumerate((y0, y1, y2, y3)):
        start = pl.multiple_of(lax.rem(c - s + 4, 4) * n, 8)
        y_ref[pl.ds(start, n), :] = ref[...]
    yb_ref[...] = y_ref[...].astype(bf16)
    for s in range(4):
        to = lax.rem(x + s, 4)
        cols = pl.ds(pl.multiple_of(lax.rem(to, 2) * 1024, 1024), 1024)
        for half in range(2):
            side = lax.rem(k + half, 2)
            kr = 2 * side + lax.div(to, 2)
            t = tn(yb_ref[:, pl.ds(pl.multiple_of(kr * NB, NB), NB)], w_ref[:, cols])
            for r in range(8):
                if half == 0:
                    own_ref[s, r] = t[:, blk(r)]
                else:
                    oth_ref[s, r] = t[:, blk(r)].astype(bf16)


def part_kernel(ids, inv_ref, s_ref, o_ref):
    x, k = ids[0], ids[1]
    kr = 2 * k + lax.div(x, 2)
    m = nn(inv_ref[:, pl.ds(pl.multiple_of(kr * NB, NB), NB)], s_ref[...], HI)
    o_ref[...] = m.reshape(64, 8, NB)


def panel_kernel(inv_ref, y_ref, o_ref):
    o_ref[...] = nt(y_ref[...], inv_ref[...], HI)


def final_kernel(scale, ids, m_ref, f_ref, o_ref, mom_ref, full_ref):
    x = ids[0]
    for cg in range(16):
        tile = None
        for kr in range(4):
            src = ((kr % 2) * 2 + cg // 8) * 16 + (kr // 2) * 8 + cg % 8
            tile = m_ref[src] if tile is None else tile + m_ref[src]
        mom_ref[:, blk(cg)] = tile * scale
    full_ref[...] = jnp.zeros((WB, WB), bf16)
    for s in range(4):
        b = lax.rem(x - s + 4, 4)
        for p, (i, j) in enumerate(PAIRS):
            full_ref[blk(i), blk(j)] = f_ref[s, p]
        cols = pl.ds(pl.multiple_of(WB * b, WB), WB)
        m = mom_ref[:, cols]
        hi = m.astype(bf16)
        rest = m - hi.astype(f32)
        mid = rest.astype(bf16)
        low = (rest - mid.astype(f32)).astype(bf16)
        full = full_ref[...]
        o_ref[:, cols] = nt(hi, full) + (nt(mid, full) + nt(low, full))


def shift(v, axis, s, n):
    return lax.ppermute(v, axis, [(i, (i + s) % n) for i in range(n)])


def everyone(v, axis, n):
    return lax.all_to_all(jnp.broadcast_to(v[None], (n,) + v.shape), axis, 0, 0, tiled=True)


def shards(calib, weight, sketch):
    tokens = calib.shape[0] * 8
    width = calib.shape[1] * 4
    hidden = weight.shape[0] * 64
    ids = jnp.stack([lax.axis_index(a) for a in ("x", "core", "row", "col")]).astype(jnp.int32)

    sketch_all = lax.all_gather(sketch, "row", axis=1, tiled=True)

    grams = call(gram_kernel, shape((8, NP + 1, 8, NB)), 1, 1, [pltpu.VMEM((WB, WB), f32)], "gram")(ids, calib)
    slab = jnp.sum(lax.all_to_all(grams, ("x", "core"), 0, 0, tiled=True), axis=0)
    trace = slab[NP]
    traces = [trace] + [shift(trace, "col", s, 4) for s in (1, 2, 3)]
    own = everyone(slab[:NP], "row", 8)
    oth = shift(own, "core", 1, 2)
    square = pltpu.VMEM((WB, WB), f32)
    diag = pltpu.VMEM((NB, NB), f32)

    def chol1(*refs):
        chol_kernel(1.0 / tokens, damping_ratio / (tokens * width), *refs)

    fac, fac_half = call(
        chol1, (shape((NP, NB, NB), bf16), shape((HALF, NB, NB), bf16)), 1, 6, [square, square, diag], "chol_gram"
    )(ids, own, oth, *traces)
    got = [shift(fac_half, "x", s, 4) for s in (1, 2, 3)]
    got_oth = [shift(v, "core", 1, 2) for v in got]
    ypart, factors = call(
        mixed_kernel,
        (shape((weight.shape[0], WB)), shape((4, NP, NB, NB), bf16)),
        1,
        9,
        [pltpu.VMEM((WB, WB), bf16)],
        "mixed",
    )(ids, fac, *got, *got_oth, sketch_all, weight)

    n = weight.shape[0] // 4
    ypieces = lax.all_to_all(ypart.reshape(4, n, WB), "col", 0, 0, tiled=True)
    tri = shape((16, HALF, 8, NB))
    cown, coth, ysum = call(cross_kernel, (tri, tri, shape((n, WB))), 1, 1, [], "cross")(ids, ypieces)
    ys = [ysum] + [shift(ysum, "col", s, 4) for s in (1, 2, 3)]
    half = cown + shift(coth, "core", 1, 2)
    piece = jnp.sum(lax.all_to_all(half, ("x", "col"), 0, 0, tiled=True), axis=0)
    piece = jnp.sum(everyone(piece, "row", 8), axis=0)
    half = everyone(piece, ("x", "col"), 16)
    coth = shift(half, "core", 1, 2)

    def chol2(*refs):
        chol2_kernel(1.0 / hidden, *refs)

    inv = call(chol2, shape((WB, WB)), 1, 2, [square, square, diag], "chol_cross")(ids, half, coth)

    town, toth, yfull = call(
        moment_kernel,
        (shape((4, 8, NB, NB)), shape((4, 8, NB, NB), bf16), shape((4 * n, WB))),
        1,
        5,
        [pltpu.VMEM((4 * n, WB), bf16)],
        "moments",
    )(ids, *ys, weight)
    t = town + shift(toth, "core", 1, 2).astype(f32)
    tile = t[0]
    for s in (1, 2, 3):
        tile = tile + shift(t[s].astype(bf16), "x", s, 4).astype(f32)
    tile = lax.psum_scatter(tile, "row", scatter_dimension=0, tiled=True)[0]

    parts = call(part_kernel, shape((64, 8, NB)), 1, 2, [], "project")(ids, inv, tile)
    parts = lax.all_to_all(parts, ("x", "core", "row"), 0, 0, tiled=True)

    def final(*refs):
        final_kernel(1.0 / math.sqrt(hidden), *refs)

    projections = call(
        final, shape((8, 4 * WB)), 1, 2, [pltpu.VMEM((8, 4 * WB), f32), pltpu.VMEM((WB, WB), bf16)], "final"
    )(ids, parts, factors)
    panels = call(panel_kernel, shape((4 * n, WB)), 0, 2, [], "panels")(inv, yfull)
    return (panels, projections)


def solution(mesh):
    fine = jax.sharding.Mesh(mesh.devices.reshape(4, 2, 8, 4), ("x", "core", "row", "col"))
    return jax.shard_map(
        shards,
        mesh=fine,
        in_specs=(P(("x", "core"), "col"), P(("x", "core", "row"), "col"), P("col", "row")),
        out_specs=(P(("x", "core", "row"), None), P(("x", "core", "row"), "col")),
        check_vma=False,
    )
```

time: 1160 us -> 254 us (0.22); the launches traced: 1150 us -> 254 us
  waiting for transfers between devices: 502 us -> 39.5 us
  other arithmetic: 454 us -> 4.34 us
  Pallas kernels: 0 us -> 66.3 us
  matrix products: 48.4 us -> 0 us
  local copies, waits for them, and re-layouts: 49 us -> 18.1 us
  starting transfers between devices: 0.42 us -> 29.4 us
    another operation x36 -> x2, other arithmetic: 434 us -> 0.53 us  [the longest x16 310 us: shards(): factor = jnp.linalg.cholesky(gram).astype(jnp.bfloat16)]
    psum x2 -> x0, waiting for transfers between devices: 235 us -> none  [the longest x1 187 us: shards(): cross = lax.psum(local_cross, ('dp', 'row')) / hidden]
    unnamed x7 -> x2, waiting for transfers between devices: 192 us -> 0.7 us
    all_to_all x0 -> x5, blocking collectives: none -> 82.3 us  [the longest x3 51.8 us: everyone(): lax.all_to_all(jnp.broadcast_to(v[None], (n,) + v.shape), axis, 0, 0, til...]
    psum x1 -> x0, blocking collectives: 75 us -> none  [shards(): total = lax.psum(local_trace, ('dp', 'row', 'col'))]
    pallas_call x0 -> x9, Pallas kernels: none -> 66.3 us  [the longest x1 30.8 us: shards(): call(chol1, (shape((NP, NB, NB), bf16), shape((HALF, NB, NB), bf16)), 1,...]
    all_gather x2 -> x1, waiting for transfers between devices: 38.9 us -> 0.01 us  [shards(): sketch_all = lax.all_gather(sketch, 'row', axis=1, tiled=True)]
    reduce_scatter x1, waiting for transfers between devices: 36.4 us -> 0.02 us  [shards(): tile = lax.psum_scatter(tile, 'row', scatter_dimension=0, tiled=True)[0]]
  transfers between devices with their start and end apart: 6 -> 23, of which waited for: 5 -> 12; matrix products, arithmetic and copies ran while one was open for 1% -> 3% of each run, Pallas kernels for 0% -> 22%
where the time goes in v1:
time: 254 us
  blocking collectives  82.3 us (32%)
  Pallas kernels  66.3 us (26%)
  waiting for transfers between devices  39.5 us (16%)
  starting transfers between devices  29.4 us (12%)
  local copies, waits for them, and re-layouts  18.1 us (7%)
  between operations  14.5 us (6%)
  other arithmetic  4.34 us (2%)
    all_to_all x3, blocking collectives, everyone(): lax.all_to_all(jnp.broadcast_to(v[None], (n,) + v.shape), axis, 0, 0, til...  51.8 us
    pallas_call x1, Pallas kernels, shards(): call(chol1, (shape((NP, NB, NB), bf16), shape((HALF, NB, NB), bf16)), 1,...  30.8 us
    ppermute x19, waiting for transfers between devices, shift(): return lax.ppermute(v, axis, [(i, (i + s) % n) for i in range(n)])  26.2 us
    pallas_call x1, Pallas kernels, shards(): call(chol2, shape((WB, WB)), 1, 2, [square, square, diag], 'chol_cross')  19.8 us
    all_to_all x1, blocking collectives, shards(): ypieces = lax.all_to_all(ypart.reshape(4, n, WB), 'col', 0, 0, tiled=True)  17.8 us
    ppermute x19, starting transfers between devices, shift(): return lax.ppermute(v, axis, [(i, (i + s) % n) for i in range(n)])  17.5 us
    unnamed x40, local copies, waits for them, and re-layouts  14.2 us
    all_to_all x1, blocking collectives, shards(): lax.all_to_all(grams, ('x', 'core'), 0, 0, tiled=True)  12.7 us
  transfers between devices with their start and end apart: 23, of which 12 were waited for; matrix products, arithmetic and copies ran while one was open for 3% of the time, Pallas kernels for 22%

profile of v1, /device:TPU:8, one launch (start us, length us, event | category | flops | bytes accessed | tf_op | source)
XLA Modules:
  0.0 254.4 jit_solution(6551823162988391695)
XLA Ops:
  8.0 1.6 copy-done.2
  9.6 1.8 gram.1
  11.4 12.7 %all_to_all.35 = f32[8,11,8,128]{3,2,1,0:T(8,128)S(1)} all-to-all(f32[8,11,8,128]{3,2,1,0:T(8,128)S(1)} %gram.1), channel_id=1, replica_groups=mesh['x'=4,'core'=2,'row'=8,'col'=4] {'x','core'}, dimensions={0} | all-to-all | bytes 720896 | tf_op jit(solution)/shard_map/all_to_all | solution.py:297
  24.2 25.4 %all_to_all.36.refs_1_ = f32[8,10,8,128]{3,2,1,0:T(8,128)S(1)} all-to-all(f32[8,10,8,128]{3,2,1,0:T(8,128)S(1)} %broadcast_in_dim.6), channel_id=1, replica_groups=mesh['x'=4,'core'=2,'row'=8,'col'=4] {'row'}, dimensions={0} | all-to-all | bytes 655360 | tf_op jit(solution)/shard_map/all_to_all | solution.py:285
  52.2 2.6 %collective-permute-start.3 = (f32[8,128]{1,0:T(8,128)S(1)}, f32[8,128]{1,0:T(8,128)S(1)}, u32[]{:S(2)}, u32[]{:S(2)}) collective-permute-start(f32[8,128]{1,0:T(8,128)S(1)} %slice_bitcast_fusion.4.refs_3_), channel_id=1, source_target_pairs={{0,3},{1,0},{2,1},{3,2},{4,7},{5,4},{6,5},{7,6},{8,11},{9,8},{10,9... | collective-permute-start | bytes 12296 | tf_op jit(solution)/shard_map/ppermute | solution.py:281
  56.2 30.8 %chol_gram.1 = (bf16[10,128,128]{2,1,0:T(8,128)(2,1)S(1)}, bf16[5,128,128]{2,1,0:T(8,128)(2,1)S(1)}) custom-call(s32[4]{0:T(128)S(1)} %pad_add_fusion.ids.refs_0_, f32[8,10,8,128]{3,2,1,0:T(8,128)S(1)} %all_to_all.36.refs_1_, f32[8,10,8,128]{3,2,1,0:T(8,128)S(1)} %collective-permute-done.refs_2_, f32[8,128]{1,0:T(8,128)S(1)} %slice_bitcast_fusion.4.refs_3_, ...), custom_call_target="tpu_custom_call" | custom-call | tf_op jit(solution)/shard_map/chol_gram/pallas_call | solution.py:308
  88.3 1.7 collective-permute-start.5
  91.1 7.1 %collective-permute-done.4.r1 = bf16[5,128,128]{2,1,0:T(8,128)(2,1)S(1)} collective-permute-done((bf16[5,128,128]{2,1,0:T(8,128)(2,1)S(1)}, bf16[5,128,128]{2,1,0:T(8,128)(2,1)S(1)}, u32[]{:S(2)}, u32[]{:S(2)}) %collective-permute-start.4) | collective-permute-done | bytes 163872 | tf_op jit(solution)/shard_map/ppermute | solution.py:281
  98.8 2.9 %copy.7.sk_ref = bf16[2048,512]{1,0:T(8,128)(2,1)S(1)} copy(bf16[2048,512]{0,1:T(8,128)(2,1)} %all-gather.2.cloned.1.call-done) | data formatting | bytes 4194304 | tf_op jit(solution)/shard_map/all_gather | solution.py:294
  111.6 3.2 %mixed.1 = (f32[416,512]{1,0:T(8,128)S(1)}, bf16[4,10,128,128]{3,2,1,0:T(8,128)(2,1)S(1)}) custom-call(s32[4]{0:T(128)S(1)} %pad_add_fusion.ids.refs_0_, bf16[10,128,128]{2,1,0:T(8,128)(2,1)S(1)} %copy-done.6, bf16[5,128,128]{2,1,0:T(8,128)(2,1)S(1)} %copy-done.8, bf16[5,128,128]{2,1,0:T(8,128)(2,1)S(1)} %copy-done.10, bf16[5,128,128]{2,1,0:T(8,128)(2,1)S(1)} %copy-done.12, ...), custom_call_target="tpu_custom_call" | custom-call | tf_op jit(solution)/shard_map/mixed/pallas_call | solution.py:313
  114.9 17.8 %all_to_all.37.y_ref = f32[4,104,512]{2,1,0:T(8,128)S(1)} all-to-all(f32[4,104,512]{2,1,0:T(8,128)S(1)} %bitcast.22), channel_id=1, replica_groups=mesh['x'=4,'core'=2,'row'=8,'col'=4] {'col'}, dimensions={0} | all-to-all | bytes 1703936 | tf_op jit(solution)/shard_map/all_to_all | solution.py:323
  132.7 1.6 cross.1
  134.7 3.1 %collective-permute-start.13 = (f32[104,512]{1,0:T(8,128)S(1)}, f32[104,512]{1,0:T(8,128)S(1)}, u32[]{:S(2)}, u32[]{:S(2)}) collective-permute-start(f32[104,512]{1,0:T(8,128)S(1)} %get-tuple-element.17.y0), channel_id=1, source_target_pairs={{0,2},{1,3},{2,0},{3,1},{4,6},{5,7},{6,4},{7,5},{8,10},{9,11},{10,... | collective-permute-start | bytes 638984 | tf_op jit(solution)/shard_map/ppermute | solution.py:281
  138.4 4.1 %collective-permute-done.12.y1 = f32[104,512]{1,0:T(8,128)S(1)} collective-permute-done((f32[104,512]{1,0:T(8,128)S(1)}, f32[104,512]{1,0:T(8,128)S(1)}, u32[]{:S(2)}, u32[]{:S(2)}) %collective-permute-start.12) | collective-permute-done | bytes 213024 | tf_op jit(solution)/shard_map/ppermute | solution.py:281
  142.5 1.9 collective-permute-done.13.y2
  144.4 2.4 collective-permute-done.14.y3
  146.8 2.0 moments.1
  149.4 2.1 collective-permute-done.15
  153.1 3.6 %collective-permute-start.17 = (bf16[8,128,128]{2,1,0:T(8,128)(2,1)}, bf16[8,128,128]{2,1,0:T(8,128)(2,1)}, u32[]{:S(2)}, u32[]{:S(2)}) collective-permute-start(bf16[8,128,128]{2,1,0:T(8,128)(2,1)} %get-tuple-element.26), channel_id=1, source_target_pairs={{0,128},{64,192},{128,0},{192,64},{1,129},{65,193},{129,1},{193,65... | collective-permute-start | bytes 786440 | tf_op jit(solution)/shard_map/ppermute | solution.py:281
  157.5 7.2 %all-to-all-start.3 = ((f32[16,5,8,128]{3,2,1,0:T(8,128)}), f32[16,5,8,128]{3,2,1,0:T(8,128)}, u32[]{:S(2)}, u32[]{:S(2)}) async-start(f32[16,5,8,128]{3,2,1,0:T(8,128)} %add.17), calls=%async_computation.3 | async-start | bytes 655360 | tf_op jit(solution)/shard_map/all_to_all | solution.py:328
  164.7 5.0 %collective-permute-done.17 = bf16[8,128,128]{2,1,0:T(8,128)(2,1)} collective-permute-done((bf16[8,128,128]{2,1,0:T(8,128)(2,1)}, bf16[8,128,128]{2,1,0:T(8,128)(2,1)}, u32[]{:S(2)}, u32[]{:S(2)}) %collective-permute-start.17) | collective-permute-done | bytes 262176 | tf_op jit(solution)/shard_map/ppermute | solution.py:281
  170.2 2.0 fusion.2
  172.2 2.9 %all-to-all-done.3 = f32[16,5,8,128]{3,2,1,0:T(8,128)} async-done(((f32[16,5,8,128]{3,2,1,0:T(8,128)}), f32[16,5,8,128]{3,2,1,0:T(8,128)}, u32[]{:S(2)}, u32[]{:S(2)}) %all-to-all-start.3) | async-done | bytes 327712 | tf_op jit(solution)/shard_map/all_to_all | solution.py:328
  176.2 13.5 %all_to_all.38 = f32[8,5,8,128]{3,2,1,0:T(8,128)S(1)} all-to-all(f32[8,5,8,128]{3,2,1,0:T(8,128)S(1)} %broadcast_in_dim.7), channel_id=1, replica_groups=mesh['x'=4,'core'=2,'row'=8,'col'=4] {'row'}, dimensions={0} | all-to-all | bytes 327680 | tf_op jit(solution)/shard_map/all_to_all | solution.py:285
  189.7 12.9 %all_to_all.39.refs_1_ = f32[16,5,8,128]{3,2,1,0:T(8,128)S(1)} all-to-all(f32[16,5,8,128]{3,2,1,0:T(8,128)S(1)} %broadcast_in_dim.8), channel_id=1, replica_groups=mesh['x'=4,'core'=2,'row'=8,'col'=4] {'x','col'}, dimensions={0} | all-to-all | bytes 655360 | tf_op jit(solution)/shard_map/all_to_all | solution.py:285
  202.6 1.6 collective-permute-done.11.refs_2_
  204.2 19.8 %chol_cross.1.inv_ref = f32[512,512]{1,0:T(8,128)S(1)} custom-call(s32[4]{0:T(128)S(1)} %pad_add_fusion.ids.refs_0_, f32[16,5,8,128]{3,2,1,0:T(8,128)S(1)} %all_to_all.39.refs_1_, f32[16,5,8,128]{3,2,1,0:T(8,128)S(1)} %collective-permute-done.11.refs_2_), custom_call_target="tpu_custom_call" | custom-call | tf_op jit(solution)/shard_map/chol_cross/pallas_call | solution.py:336
  224.8 1.6 project.1
  226.5 4.6 %all-to-all-start.6 = ((f32[64,8,128]{2,1,0:T(8,128)}), f32[64,8,128]{2,1,0:T(8,128)S(1)}, u32[]{:S(2)}, u32[]{:S(2)}) async-start(f32[64,8,128]{2,1,0:T(8,128)} %project.1), calls=%async_computation.7 | async-start | bytes 524288 | tf_op jit(solution)/shard_map/all_to_all | solution.py:353
  232.2 2.5 panels.1
  234.7 9.6 %all-to-all-done.6.refs_1_ = f32[64,8,128]{2,1,0:T(8,128)S(1)} async-done(((f32[64,8,128]{2,1,0:T(8,128)}), f32[64,8,128]{2,1,0:T(8,128)S(1)}, u32[]{:S(2)}, u32[]{:S(2)}) %all-to-all-start.6) | async-done | bytes 262176 | tf_op jit(solution)/shard_map/all_to_all | solution.py:353
  244.3 3.1 %final.1 = f32[8,2048]{1,0:T(8,128)} custom-call(s32[4]{0:T(128)S(1)} %pad_add_fusion.ids.refs_0_, f32[64,8,128]{2,1,0:T(8,128)S(1)} %all-to-all-done.6.refs_1_, bf16[4,10,128,128]{3,2,1,0:T(8,128)(2,1)S(1)} %get-tuple-element.21.refs_2_), custom_call_target="tpu_custom_call" | custom-call | tf_op jit(solution)/shard_map/final/pallas_call | solution.py:358
  (84 shorter events, 25.1 us)
Async XLA Ops:
  7.2 91.6 %all-gather.2.cloned.1.call-start = ((), (), s32[]{:S(2)}) async-start(), calls=%async_computation.8 | async-start | bytes 2359296 | tf_op jit(solution)/shard_map/all_gather | solution.py:294
  8.0 1.6 copy-start.2
  49.6 6.6 %collective-permute-start = (f32[8,10,8,128]{3,2,1,0:T(8,128)S(1)}, f32[8,10,8,128]{3,2,1,0:T(8,128)S(1)}, u32[]{:S(2)}, u32[]{:S(2)}) collective-permute-start(f32[8,10,8,128]{3,2,1,0:T(8,128)S(1)} %all_to_all.36.refs_1_), channel_id=1, source_target_pairs={{0,32},{32,0},{1,33},{33,1},{2,34},{34,2},{3,35},{35,3},{4,36},{36... | collective-permute-start | bytes 983048 | tf_op jit(solution)/shard_map/ppermute | solution.py:281
  49.6 5.2 %collective-permute-start.1 = (f32[8,128]{1,0:T(8,128)S(1)}, f32[8,128]{1,0:T(8,128)S(1)}, u32[]{:S(2)}, u32[]{:S(2)}) collective-permute-start(f32[8,128]{1,0:T(8,128)S(1)} %slice_bitcast_fusion.4.refs_3_), channel_id=1, source_target_pairs={{0,1},{1,2},{2,3},{3,0},{4,5},{5,6},{6,7},{7,4},{8,9},{9,10},{10,1... | collective-permute-start | bytes 12296 | tf_op jit(solution)/shard_map/ppermute | solution.py:281
  51.1 5.1 %collective-permute-start.2 = (f32[8,128]{1,0:T(8,128)S(1)}, f32[8,128]{1,0:T(8,128)S(1)}, u32[]{:S(2)}, u32[]{:S(2)}) collective-permute-start(f32[8,128]{1,0:T(8,128)S(1)} %slice_bitcast_fusion.4.refs_3_), channel_id=1, source_target_pairs={{0,2},{1,3},{2,0},{3,1},{4,6},{5,7},{6,4},{7,5},{8,10},{9,11},{10,... | collective-permute-start | bytes 12296 | tf_op jit(solution)/shard_map/ppermute | solution.py:281
  52.2 4.1 %collective-permute-start.3 = (f32[8,128]{1,0:T(8,128)S(1)}, f32[8,128]{1,0:T(8,128)S(1)}, u32[]{:S(2)}, u32[]{:S(2)}) collective-permute-start(f32[8,128]{1,0:T(8,128)S(1)} %slice_bitcast_fusion.4.refs_3_), channel_id=1, source_target_pairs={{0,3},{1,0},{2,1},{3,2},{4,7},{5,4},{6,5},{7,6},{8,11},{9,8},{10,9... | collective-permute-start | bytes 12296 | tf_op jit(solution)/shard_map/ppermute | solution.py:281
  87.8 10.3 %collective-permute-start.4 = (bf16[5,128,128]{2,1,0:T(8,128)(2,1)S(1)}, bf16[5,128,128]{2,1,0:T(8,128)(2,1)S(1)}, u32[]{:S(2)}, u32[]{:S(2)}) collective-permute-start(bf16[5,128,128]{2,1,0:T(8,128)(2,1)S(1)} %get-tuple-element.13), channel_id=1, source_target_pairs={{0,64},{64,128},{128,192},{192,0},{1,65},{65,129},{129,193},{193,1... | collective-permute-start | bytes 491528 | tf_op jit(solution)/shard_map/ppermute | solution.py:281
  88.3 9.8 %collective-permute-start.5 = (bf16[5,128,128]{2,1,0:T(8,128)(2,1)S(1)}, bf16[5,128,128]{2,1,0:T(8,128)(2,1)S(1)}, u32[]{:S(2)}, u32[]{:S(2)}) collective-permute-start(bf16[5,128,128]{2,1,0:T(8,128)(2,1)S(1)} %get-tuple-element.13), channel_id=1, source_target_pairs={{0,128},{64,192},{128,0},{192,64},{1,129},{65,193},{129,1},{193,65... | collective-permute-start | bytes 491528 | tf_op jit(solution)/shard_map/ppermute | solution.py:281
  90.0 8.7 %collective-permute-start.6 = (bf16[5,128,128]{2,1,0:T(8,128)(2,1)S(1)}, bf16[5,128,128]{2,1,0:T(8,128)(2,1)S(1)}, u32[]{:S(2)}, u32[]{:S(2)}) collective-permute-start(bf16[5,128,128]{2,1,0:T(8,128)(2,1)S(1)} %get-tuple-element.13), channel_id=1, source_target_pairs={{0,192},{64,0},{128,64},{192,128},{1,193},{65,1},{129,65},{193,129... | collective-permute-start | bytes 491528 | tf_op jit(solution)/shard_map/ppermute | solution.py:281
  98.1 4.9 %copy-start.7 = (bf16[5,128,128]{2,1,0:T(8,128)(2,1)}, bf16[5,128,128]{2,1,0:T(8,128)(2,1)S(1)}, u32[]{:S(2)}) copy-start(bf16[5,128,128]{2,1,0:T(8,128)(2,1)S(1)} %collective-permute-done.4.r1) | copy-start | bytes 491524
  98.1 3.6 %collective-permute-start.7 = (bf16[5,128,128]{2,1,0:T(8,128)(2,1)S(1)}, bf16[5,128,128]{2,1,0:T(8,128)(2,1)S(1)}, u32[]{:S(2)}, u32[]{:S(2)}) collective-permute-start(bf16[5,128,128]{2,1,0:T(8,128)(2,1)S(1)} %collective-permute-done.4.r1), channel_id=1, source_target_pairs={{0,32},{32,0},{1,33},{33,1},{2,34},{34,2},{3,35},{35,3},{4,36},{36... | collective-permute-start | bytes 491528 | tf_op jit(solution)/shard_map/ppermute | solution.py:281
  98.1 4.9 %copy-start.9 = (bf16[5,128,128]{2,1,0:T(8,128)(2,1)}, bf16[5,128,128]{2,1,0:T(8,128)(2,1)S(1)}, u32[]{:S(2)}) copy-start(bf16[5,128,128]{2,1,0:T(8,128)(2,1)S(1)} %collective-permute-done.5.r2) | copy-start | bytes 491524
  98.1 4.2 %collective-permute-start.8 = (bf16[5,128,128]{2,1,0:T(8,128)(2,1)S(1)}, bf16[5,128,128]{2,1,0:T(8,128)(2,1)S(1)}, u32[]{:S(2)}, u32[]{:S(2)}) collective-permute-start(bf16[5,128,128]{2,1,0:T(8,128)(2,1)S(1)} %collective-permute-done.5.r2), channel_id=1, source_target_pairs={{0,32},{32,0},{1,33},{33,1},{2,34},{34,2},{3,35},{35,3},{4,36},{36... | collective-permute-start | bytes 491528 | tf_op jit(solution)/shard_map/ppermute | solution.py:281
  98.7 4.3 %copy-start.11 = (bf16[5,128,128]{2,1,0:T(8,128)(2,1)}, bf16[5,128,128]{2,1,0:T(8,128)(2,1)S(1)}, u32[]{:S(2)}) copy-start(bf16[5,128,128]{2,1,0:T(8,128)(2,1)S(1)} %collective-permute-done.6.r3) | copy-start | bytes 491524
  98.7 4.3 %collective-permute-start.9 = (bf16[5,128,128]{2,1,0:T(8,128)(2,1)S(1)}, bf16[5,128,128]{2,1,0:T(8,128)(2,1)S(1)}, u32[]{:S(2)}, u32[]{:S(2)}) collective-permute-start(bf16[5,128,128]{2,1,0:T(8,128)(2,1)S(1)} %collective-permute-done.6.r3), channel_id=1, source_target_pairs={{0,32},{32,0},{1,33},{33,1},{2,34},{34,2},{3,35},{35,3},{4,36},{36... | collective-permute-start | bytes 491528 | tf_op jit(solution)/shard_map/ppermute | solution.py:281
  103.7 1.5 copy-start
  105.2 1.0 copy-start.6
  114.9 32.0 %copy-start.1 = (bf16[416,2048]{1,0:T(8,128)(2,1)S(1)}, bf16[416,2048]{1,0:T(8,128)(2,1)}, u32[]{:S(2)}) copy-start(bf16[416,2048]{1,0:T(8,128)(2,1)} %w_ref.3) | copy-start | bytes 5111812
  134.2 8.3 %collective-permute-start.12 = (f32[104,512]{1,0:T(8,128)S(1)}, f32[104,512]{1,0:T(8,128)S(1)}, u32[]{:S(2)}, u32[]{:S(2)}) collective-permute-start(f32[104,512]{1,0:T(8,128)S(1)} %get-tuple-element.17.y0), channel_id=1, source_target_pairs={{0,1},{1,2},{2,3},{3,0},{4,5},{5,6},{6,7},{7,4},{8,9},{9,10},{10,1... | collective-permute-start | bytes 638984 | tf_op jit(solution)/shard_map/ppermute | solution.py:281
  134.7 9.7 %collective-permute-start.13 = (f32[104,512]{1,0:T(8,128)S(1)}, f32[104,512]{1,0:T(8,128)S(1)}, u32[]{:S(2)}, u32[]{:S(2)}) collective-permute-start(f32[104,512]{1,0:T(8,128)S(1)} %get-tuple-element.17.y0), channel_id=1, source_target_pairs={{0,2},{1,3},{2,0},{3,1},{4,6},{5,7},{6,4},{7,5},{8,10},{9,11},{10,... | collective-permute-start | bytes 638984 | tf_op jit(solution)/shard_map/ppermute | solution.py:281
  137.8 9.0 %collective-permute-start.14 = (f32[104,512]{1,0:T(8,128)S(1)}, f32[104,512]{1,0:T(8,128)S(1)}, u32[]{:S(2)}, u32[]{:S(2)}) collective-permute-start(f32[104,512]{1,0:T(8,128)S(1)} %get-tuple-element.17.y0), channel_id=1, source_target_pairs={{0,3},{1,0},{2,1},{3,2},{4,7},{5,4},{6,5},{7,6},{8,11},{9,8},{10,9... | collective-permute-start | bytes 638984 | tf_op jit(solution)/shard_map/ppermute | solution.py:281
  148.8 3.2 %copy-start.3 = (f32[416,512]{1,0:T(8,128)}, f32[416,512]{1,0:T(8,128)S(1)}, u32[]{:S(2)}) copy-start(f32[416,512]{1,0:T(8,128)S(1)} %get-tuple-element.18.y_ref) | copy-start | bytes 2555908
  148.8 2.7 %collective-permute-start.15 = (bf16[4,8,128,128]{3,2,1,0:T(8,128)(2,1)S(1)}, bf16[4,8,128,128]{3,2,1,0:T(8,128)(2,1)S(1)}, u32[]{:S(2)}, u32[]{:S(2)}) collective-permute-start(bf16[4,8,128,128]{3,2,1,0:T(8,128)(2,1)S(1)} %get-tuple-element.20), channel_id=1, source_target_pairs={{0,32},{32,0},{1,33},{33,1},{2,34},{34,2},{3,35},{35,3},{4,36},{36... | collective-permute-start | bytes 3145736 | tf_op jit(solution)/shard_map/ppermute | solution.py:281
  148.9 7.8 %collective-permute-start.10 = (f32[16,5,8,128]{3,2,1,0:T(8,128)S(1)}, f32[16,5,8,128]{3,2,1,0:T(8,128)S(1)}, u32[]{:S(2)}, u32[]{:S(2)}) collective-permute-start(f32[16,5,8,128]{3,2,1,0:T(8,128)S(1)} %get-tuple-element.16), channel_id=1, source_target_pairs={{0,32},{32,0},{1,33},{33,1},{2,34},{34,2},{3,35},{35,3},{4,36},{36... | collective-permute-start | bytes 983048 | tf_op jit(solution)/shard_map/ppermute | solution.py:281
  152.9 11.8 %collective-permute-start.16 = (bf16[8,128,128]{2,1,0:T(8,128)(2,1)}, bf16[8,128,128]{2,1,0:T(8,128)(2,1)}, u32[]{:S(2)}, u32[]{:S(2)}) collective-permute-start(bf16[8,128,128]{2,1,0:T(8,128)(2,1)} %get-tuple-element.24), channel_id=1, source_target_pairs={{0,64},{64,128},{128,192},{192,0},{1,65},{65,129},{129,193},{193,1... | collective-permute-start | bytes 786440 | tf_op jit(solution)/shard_map/ppermute | solution.py:281
  153.1 16.6 %collective-permute-start.17 = (bf16[8,128,128]{2,1,0:T(8,128)(2,1)}, bf16[8,128,128]{2,1,0:T(8,128)(2,1)}, u32[]{:S(2)}, u32[]{:S(2)}) collective-permute-start(bf16[8,128,128]{2,1,0:T(8,128)(2,1)} %get-tuple-element.26), channel_id=1, source_target_pairs={{0,128},{64,192},{128,0},{192,64},{1,129},{65,193},{129,1},{193,65... | collective-permute-start | bytes 786440 | tf_op jit(solution)/shard_map/ppermute | solution.py:281
  156.7 13.5 %collective-permute-start.18 = (bf16[8,128,128]{2,1,0:T(8,128)(2,1)}, bf16[8,128,128]{2,1,0:T(8,128)(2,1)}, u32[]{:S(2)}, u32[]{:S(2)}) collective-permute-start(bf16[8,128,128]{2,1,0:T(8,128)(2,1)} %get-tuple-element.25), channel_id=1, source_target_pairs={{0,192},{64,0},{128,64},{192,128},{1,193},{65,1},{129,65},{193,129... | collective-permute-start | bytes 786440 | tf_op jit(solution)/shard_map/ppermute | solution.py:281
  157.5 17.7 %all-to-all-start.3 = ((f32[16,5,8,128]{3,2,1,0:T(8,128)}), f32[16,5,8,128]{3,2,1,0:T(8,128)}, u32[]{:S(2)}, u32[]{:S(2)}) async-start(f32[16,5,8,128]{3,2,1,0:T(8,128)} %add.17), calls=%async_computation.3 | async-start | bytes 655360 | tf_op jit(solution)/shard_map/all_to_all | solution.py:328
  164.7 59.3 %reduce-scatter.2.cloned.1.call-start = ((), (), s32[]{:S(2)}) async-start(), calls=%async_computation.9 | async-start | bytes 589824 | tf_op jit(solution)/shard_map/reduce_scatter | solution.py:350
  202.6 1.6 collective-permute-start.11
  226.5 17.8 %all-to-all-start.6 = ((f32[64,8,128]{2,1,0:T(8,128)}), f32[64,8,128]{2,1,0:T(8,128)S(1)}, u32[]{:S(2)}, u32[]{:S(2)}) async-start(f32[64,8,128]{2,1,0:T(8,128)} %project.1), calls=%async_computation.7 | async-start | bytes 524288 | tf_op jit(solution)/shard_map/all_to_all | solution.py:353
  231.1 1.2 copy-start.4
  (11 other events, 9.1 us)
Sparse Core Ops, SparseCore 0:
  9.8 50.2 all-gather.1
  172.3 33.6 reduce-scatter.1
